TPU v7x, 32 devices: a whole 2x2x4 slice. The times are simulated.
32 devices in a mesh: groups: 2 (over x), seq: 16 (over z, y, core).
Axes of the slice: x: 2, y: 2, z: 4, core: 2. Of those that a mesh axis runs over, the one named last changes fastest.
Arguments:
- window_queries: bfloat16 [4096, 2048], P(('groups', 'seq')), parts along dimension 0, may hold values from -300 to 300
- window_kv: bfloat16 [4096, 512], P(('groups', 'seq')), parts along dimension 0, may hold values from -6 to 6
- stream: bfloat16 [4096, 2880], P(('groups', 'seq')), parts along dimension 0, may hold values from -6 to 6
- moe_gain: float32 [2880], replicated, may hold values from 0.25 to 1.75
- routes: int32 [4096, 4], P(('groups', 'seq')), parts along dimension 0, may hold values from 0 to 15, as said below
- route_gates: float32 [4096, 4], P(('groups', 'seq')), parts along dimension 0, may hold values from 0.1 to 0.6
- gate_proj: bfloat16 [2880, 23040], P(None, 'seq'), may hold values from -0.109375 to 0.109375
- up_proj: bfloat16 [2880, 23040], P(None, 'seq'), may hold values from -0.109375 to 0.109375
- down_proj: bfloat16 [23040, 2880], P('seq'), may hold values from -0.15625 to 0.15625
- attn_gain: float32 [2880], replicated, may hold values from 0.25 to 1.75
- kv_proj: bfloat16 [2880, 512], replicated, may hold values from -0.109375 to 0.109375
- tract_queries: bfloat16 [4096, 2048], P(('groups', 'seq')), parts along dimension 0, may hold values from -300 to 300
Outputs:
- attn_window: bfloat16 [4096, 2048], P(('groups', 'seq')), parts along dimension 0
- stream_next: bfloat16 [4096, 2880], P(('groups', 'seq')), parts along dimension 0
- attn_tract: bfloat16 [4096, 2048], P(('groups', 'seq')), parts along dimension 0
There are 2 independent parts, one for each index of `groups`. A program takes and returns all parts, laid end to end along the dimension named above; an argument that names none is the same for every part. Nothing has to cross between parts.
Inputs may be any that keep to these rules, and one draw needn't show every extreme that they name: `routes`: in each device's block of 128 tokens every expert is named exactly 32 times; a token names 4 different experts.
All inputs are finite; a program needn't handle non-finite values.
Results may differ from a plain program's by a relative error of at most 0.025.
The roundings to bfloat16 on the way count: a program that leaves them out, or rounds other values in their place, can miss the bound.
Values may be sent and summed in bfloat16 or wider, within the bound.
A program may use at most 128 MiB of HBM per device.

v0:
```python
import jax
import jax.numpy as jnp
from jax import lax
from jax.sharding import PartitionSpec as P

HEADS = 32
KV_HEADS = 4
HEAD_DIM = 64
EXPERTS = 16
TOP = 4
WINDOW = 128
STRETCH = 1024


def from_behind(block, axis, distance):
    devices = range(lax.axis_size(axis))
    route = [(i - distance, i) for i in devices if i - distance in devices]
    return lax.ppermute(block, axis, route)


def normed(values, gain):
    widened = values.astype(jnp.float32)
    second = jnp.mean(widened * widened, axis=-1, keepdims=True)
    return (widened * lax.rsqrt(second + 1e-05) * gain).astype(jnp.bfloat16)


def attend(queries, keys, values, allowed):
    query_rows = queries.shape[0]
    key_rows = keys.shape[0]
    group_size = HEADS // KV_HEADS
    query_heads = queries.reshape(query_rows, KV_HEADS, group_size, HEAD_DIM)
    key_heads = keys.reshape(key_rows, KV_HEADS, HEAD_DIM)
    value_heads = values.reshape(key_rows, KV_HEADS, HEAD_DIM)
    scores = (
        jnp.einsum("qkgd,skd->kgqs", query_heads, key_heads, preferred_element_type=jnp.float32)
        * 0.125
    )
    scores = jnp.where(allowed, scores, -1e30)
    peak = jnp.max(scores, axis=-1, keepdims=True)
    weights = jnp.exp(scores - peak)
    totals = jnp.sum(weights, axis=-1)
    mixed = jnp.einsum(
        "kgqs,skd->qkgd",
        weights.astype(jnp.bfloat16),
        value_heads,
        preferred_element_type=jnp.float32,
    )
    mixed = mixed / jnp.transpose(totals, (2, 0, 1))[..., None]
    return mixed.reshape(query_rows, HEADS * HEAD_DIM).astype(jnp.bfloat16)


def on_device(
    window_queries,
    window_kv,
    stream,
    moe_gain,
    routes,
    route_gates,
    gate_proj,
    up_proj,
    down_proj,
    attn_gain,
    kv_proj,
    tract_queries,
):
    rows_here = window_queries.shape[0]
    half_cols = window_kv.shape[1] // 2
    device = lax.axis_index("seq")
    devices = lax.axis_size("seq")
    query_block = min(512, rows_here)
    first_row = device * rows_here
    rim_keys = from_behind(window_kv, "seq", 1)
    window_keys = jnp.concatenate([rim_keys, window_kv], 0)
    offset = 0
    query_pos = first_row + offset + jnp.arange(query_block, dtype=jnp.int32)
    key_pos = first_row + offset - WINDOW + jnp.arange(query_block + WINDOW, dtype=jnp.int32)
    distance = query_pos[:, None] - key_pos[None, :]
    allowed = (distance >= 0) & (distance < WINDOW) & (key_pos[None, :] >= 0)
    window_parts = attend(
        window_queries, window_keys[:, :half_cols], window_keys[:, half_cols:], allowed
    )
    moe_input = normed(stream, moe_gain)
    model_width = moe_input.shape[1]
    capacity = rows_here * TOP // EXPERTS
    split_count = devices // EXPERTS
    flat_routes = routes.reshape(-1)
    onehot = (flat_routes[:, None] == jnp.arange(EXPERTS, dtype=jnp.int32)[None, :]).astype(
        jnp.int32
    )
    slot_rank = jnp.sum(onehot * (jnp.cumsum(onehot, axis=0) - 1), axis=1)
    slot_index = flat_routes * capacity + slot_rank
    token_ids = jnp.arange(rows_here * TOP, dtype=jnp.int32) // TOP
    slot_table = jnp.zeros((EXPERTS * capacity,), jnp.int32).at[slot_index].set(token_ids)
    outgoing = moe_input[slot_table].reshape(EXPERTS, capacity, model_width)
    copies = jnp.repeat(outgoing, split_count, axis=0)
    arrived = lax.all_to_all(copies, "seq", split_axis=0, concat_axis=0, tiled=True)
    flat_rows = arrived.reshape(-1, model_width)
    gate_vals = jnp.dot(flat_rows, gate_proj, preferred_element_type=jnp.float32)
    up_vals = jnp.dot(flat_rows, up_proj, preferred_element_type=jnp.float32)
    hidden = (jax.nn.silu(gate_vals) * up_vals).astype(jnp.bfloat16)
    block_out = jnp.dot(hidden, down_proj, preferred_element_type=jnp.float32).astype(jnp.bfloat16)
    partial_value = block_out.reshape(arrived.shape)
    returned = lax.all_to_all(partial_value, "seq", split_axis=0, concat_axis=0, tiled=True)
    summed = jnp.sum(
        returned.astype(jnp.float32).reshape(EXPERTS, split_count, capacity, model_width), axis=1
    )
    summed = summed.reshape(EXPERTS * capacity, model_width)
    picked = summed[slot_index].reshape(rows_here, TOP, model_width)
    stream_next = (
        stream.astype(jnp.float32) + jnp.sum(picked * route_gates[:, :, None], axis=1)
    ).astype(jnp.bfloat16)
    attn_input = normed(stream_next, attn_gain)
    tract_kv = jnp.dot(attn_input, kv_proj, preferred_element_type=jnp.float32).astype(jnp.bfloat16)
    lead = STRETCH // 2
    back_devices = STRETCH // rows_here - 1
    earlier = []
    for shift_by in range(back_devices, 0, -1):
        earlier.append(from_behind(tract_kv, "seq", shift_by))
    context_keys = jnp.concatenate(earlier + [tract_kv], 0)
    key_pos = (
        first_row
        - back_devices * rows_here
        + jnp.arange((back_devices + 1) * rows_here, dtype=jnp.int32)
    )
    offset = 0
    query_pos = first_row + offset + jnp.arange(query_block, dtype=jnp.int32)
    allowed = (
        (key_pos[None, :] <= query_pos[:, None])
        & (key_pos[None, :] >= 0)
        & ((key_pos[None, :] + lead) // STRETCH == (query_pos[:, None] + lead) // STRETCH)
    )
    tract_parts = attend(
        tract_queries, context_keys[:, :half_cols], context_keys[:, half_cols:], allowed
    )
    return (window_parts, stream_next, tract_parts)


def solution(mesh):
    return jax.shard_map(
        on_device,
        mesh=mesh,
        in_specs=(
            P(("groups", "seq"), None),
            P(("groups", "seq"), None),
            P(("groups", "seq"), None),
            P(),
            P(("groups", "seq"), None),
            P(("groups", "seq"), None),
            P(None, "seq"),
            P(None, "seq"),
            P("seq", None),
            P(),
            P(),
            P(("groups", "seq"), None),
        ),
        out_specs=(
            P(("groups", "seq"), None),
            P(("groups", "seq"), None),
            P(("groups", "seq"), None),
        ),
        check_vma=False,
    )
```

profile of v0, /device:TPU:0, one launch (start us, length us, event | category | flops | bytes accessed | tf_op | source)
XLA Modules:
  0.0 309.2 jit_solution(2998349848496716185)
XLA Ops:
  4.2 2.4 scatter_custom_fusion
  6.7 2.3 copy.33
  10.4 2.2 fusion.18
  12.6 7.9 %gather_fusion = bf16[512,2880]{1,0:T(8,128)(2,1)} fusion(bf16[128,2880]{1,0:T(8,128)(2,1)} %fusion.18, s32[1024]{0:T(1024)S(1)} %pad_clamp_fusion.1), kind=kCustom, calls=%fused_computation | custom fusion | bytes 5900288 | tf_op jit(solution)/shard_map/gather | solution.py:94
  20.5 75.1 %all_to_all.10 = bf16[16,32,2880]{2,1,0:T(8,128)(2,1)S(1)} all-to-all(bf16[16,32,2880]{2,1,0:T(8,128)(2,1)} %bitcast.96), channel_id=1, replica_groups=mesh['groups'=2,'seq'=16] {'seq'}, dimensions={0} | all-to-all | bytes 5898240 | tf_op jit(solution)/shard_map/all_to_all | solution.py:96
  97.2 9.0 %fusion.54 = f32[512,1440]{0,1:T(8,128)} fusion(bf16[512,2880]{1,0:T(8,128)(2,1)S(1)} %bitcast.97, bf16[2880,1440]{0,1:T(8,128)(2,1)} %param.18), kind=kOutput, calls=%fused_computation.103 | convolution fusion | flops 4246732800 | bytes 14192640 | tf_op jit(solution)/shard_map/dot_general | solution.py:98
  106.2 26.3 %convolution_convert_fusion = bf16[512,2880]{0,1:T(8,128)(2,1)} fusion(bf16[1440,2880]{1,0:T(8,128)(2,1)} %param.20, bf16[512,2880]{1,0:T(8,128)(2,1)} %bitcast.98, bf16[2880,1440]{0,1:T(8,128)(2,1)} %param.19, f32[512,1440]{0,1:T(8,128)} %fusion.54), kind=kOutput, calls=%fused_computation.11 | convolution fusion | flops 8499363840 | bytes 25436160 | tf_op jit(solution)/shard_map/dot_general | solution.py:101
  132.5 4.6 %copy.38 = bf16[512,2880]{1,0:T(8,128)(2,1)} copy(bf16[512,2880]{0,1:T(8,128)(2,1)} %convolution_convert_fusion) | data formatting | bytes 5898240 | tf_op jit(solution)/shard_map/convert_element_type | solution.py:101
  137.1 4.8 %all-to-all-start.1 = ((bf16[16,32,2880]{2,1,0:T(8,128)(2,1)}), bf16[16,32,2880]{2,1,0:T(8,128)(2,1)}, u32[]{:S(2)}, u32[]{:S(2)}) async-start(bf16[16,32,2880]{2,1,0:T(8,128)(2,1)} %bitcast.95), calls=%async_computation.1 | async-start | bytes 6029312 | tf_op jit(solution)/shard_map/all_to_all | solution.py:103
  141.9 2.6 collective-permute-start
  146.4 2.0 copy.42
  148.4 2.0 copy.31
  152.6 2.0 copy-done.1
  155.5 43.6 %all-to-all-done.1 = bf16[16,32,2880]{2,1,0:T(8,128)(2,1)} async-done(((bf16[16,32,2880]{2,1,0:T(8,128)(2,1)}), bf16[16,32,2880]{2,1,0:T(8,128)(2,1)}, u32[]{:S(2)}, u32[]{:S(2)}) %all-to-all-start.1) | async-done | bytes 2949152 | tf_op jit(solution)/shard_map/all_to_all | solution.py:103
  199.1 4.8 %bitcast_convert_fusion = f32[512,2880]{1,0:T(8,128)} fusion(bf16[16,32,2880]{2,1,0:T(8,128)(2,1)} %all-to-all-done.1), kind=kLoop, calls=%fused_computation.18 | loop fusion | flops 1474560 | bytes 8847360 | tf_op jit(solution)/shard_map/reshape | solution.py:107
  203.9 9.7 %gather_fusion.1 = f32[512,2880]{1,0:T(8,128)} fusion(f32[512,2880]{1,0:T(8,128)} %bitcast_convert_fusion, s32[1024]{0:T(1024)S(1)} %pad_clamp_fusion), kind=kCustom, calls=%fused_computation.1 | custom fusion | bytes 11798528 | tf_op jit(solution)/shard_map/gather | solution.py:108
  213.6 7.7 %reshape.220 = f32[128,4,2880]{2,1,0:T(4,128)} reshape(f32[512,2880]{1,0:T(8,128)} %gather_fusion.1) | data formatting | bytes 11796480 | tf_op jit(solution)/shard_map/reshape | solution.py:108
  221.3 7.2 %multiply_reduce_fusion = f32[128,2880]{1,0:T(8,128)S(1)} fusion(f32[128,4,2880]{2,1,0:T(4,128)} %reshape.220, f32[128,4]{1,0:T(8,128)S(1)} %copy-done.7), kind=kLoop, calls=%fused_computation.10 | loop fusion | flops 2580480 | bytes 7374848 | tf_op jit(solution)/shard_map/reduce_sum | solution.py:110
  230.3 19.7 %collective-permute-start.1 = (bf16[128,512]{1,0:T(8,128)(2,1)S(1)}, bf16[128,512]{1,0:T(8,128)(2,1)}, u32[]{:S(2)}, u32[]{:S(2)}) collective-permute-start(bf16[128,512]{1,0:T(8,128)(2,1)S(1)} %convolution_convert_fusion.1), channel_id=1, source_target_pairs={{0,7},{1,8},{2,9},{3,10},{4,11},{5,12},{6,13},{7,14},{8,15},{16,23... | collective-permute-start | bytes 393224 | tf_op jit(solution)/shard_map/ppermute | solution.py:18
  251.5 1.9 divide_convert_fusion.1
  253.4 2.0 copy.44
  255.4 1.9 collective-permute-start.3
  257.4 1.9 collective-permute-start.4
  259.3 5.9 %collective-permute-start.5 = (bf16[128,512]{1,0:T(8,128)(2,1)S(1)}, bf16[128,512]{1,0:T(8,128)(2,1)S(1)}, u32[]{:S(2)}, u32[]{:S(2)}) collective-permute-start(bf16[128,512]{1,0:T(8,128)(2,1)S(1)} %convolution_convert_fusion.1), channel_id=1, source_target_pairs={{0,3},{1,4},{2,5},{3,6},{4,7},{5,8},{6,9},{7,10},{8,11},{9,12},{10... | collective-permute-start | bytes 393224 | tf_op jit(solution)/shard_map/ppermute | solution.py:18
  265.2 2.3 copy.45
  269.7 2.6 collective-permute-start.7
  275.4 2.0 copy.41
  277.4 2.0 copy.40
  279.5 9.3 %fusion.2 = (f32[4,8,128]{2,1,0:T(8,128)S(1)}, f32[4,1024,128,8]{2,1,3,0:T(8,128)}) fusion(pred[128,1024]{0,1:T(8,128)(4,1)S(1)} %compare_and_fusion, bf16[1024,4,64,1]{0,2,3,1:T(8,128)(2,1)} %bitcast.101, bf16[128,4,8,64]{0,3,2,1:T(8,128)(2,1)} %bitcast.99), kind=kOutput, calls=%fused_computation.7 | convolution fusion | flops 549449728 | bytes 17973248 | tf_op jit(solution)/shard_map/qkgd,skd->kgqs/dot_general | solution.py:35
  288.8 9.4 %fusion = f32[4,8,128]{2,1,0:T(8,128)S(1)} fusion(f32[4,1024,128,8]{2,1,3,0:T(8,128)} %get-tuple-element.18, f32[4,8,128]{2,1,0:T(8,128)S(1)} %get-tuple-element.17, pred[128,1024]{0,1:T(8,128)(4,1)S(1)} %compare_and_fusion), kind=kLoop, calls=%fused_computation.5 | loop fusion | flops 16773120 | bytes 16941056 | tf_op jit(solution)/shard_map/reduce_sum | solution.py:41
  298.1 8.6 %divide_convert_fusion = bf16[128,4,8,64]{0,3,2,1:T(8,128)(2,1)} fusion(bf16[1024,4,64,1]{0,2,3,1:T(8,128)(2,1)S(1)} %bitcast.103, f32[4,1024,128,8]{2,1,3,0:T(8,128)} %get-tuple-element.18, f32[4,8,128]{2,1,0:T(8,128)S(1)} %get-tuple-element.17, pred[128,1024]{0,1:T(8,128)(4,1)S(1)} %compare_and_fusion, f32[128,4,8]{0,2,1:T(8,128)S(1)} %bitcast.108), kind=kOutput, calls=%fused_computation.37 | convolution fusion | flops 554172416 | bytes 17989632 | tf_op jit(solution)/shard_map/kgqs,skd->qkgd/dot_general | solution.py:42
  306.7 2.0 copy.46
  (77 shorter events, 19.9 us)
Async XLA Ops:
  0.6 229.0 %copy-start = (bf16[2880,512]{1,0:T(8,128)(2,1)S(1)}, bf16[2880,512]{1,0:T(8,128)(2,1)}, u32[]{:S(2)}) copy-start(bf16[2880,512]{1,0:T(8,128)(2,1)} %param.22) | copy-start | bytes 8847364
  95.6 1.6 copy-start.4
  137.1 4.8 %copy-start.8 = (bf16[128,512]{1,0:T(8,128)(2,1)S(1)}, bf16[128,512]{1,0:T(8,128)(2,1)}, u32[]{:S(2)}) copy-start(bf16[128,512]{1,0:T(8,128)(2,1)} %param.13) | copy-start | bytes 393220
  137.1 8.5 %copy-start.9 = (f32[128,4]{0,1:T(4,128)S(1)}, f32[128,4]{0,1:T(4,128)}, u32[]{:S(2)}) copy-start(f32[128,4]{0,1:T(4,128)} %param.17) | copy-start | bytes 6148
  137.1 62.0 %all-to-all-start.1 = ((bf16[16,32,2880]{2,1,0:T(8,128)(2,1)}), bf16[16,32,2880]{2,1,0:T(8,128)(2,1)}, u32[]{:S(2)}, u32[]{:S(2)}) async-start(bf16[16,32,2880]{2,1,0:T(8,128)(2,1)} %bitcast.95), calls=%async_computation.1 | async-start | bytes 6029312 | tf_op jit(solution)/shard_map/all_to_all | solution.py:103
  141.9 8.5 %collective-permute-start = (bf16[128,512]{1,0:T(8,128)(2,1)S(1)}, bf16[128,512]{1,0:T(8,128)(2,1)S(1)}, u32[]{:S(2)}, u32[]{:S(2)}) collective-permute-start(bf16[128,512]{1,0:T(8,128)(2,1)S(1)} %copy-done.8), channel_id=1, source_target_pairs={{0,1},{1,2},{2,3},{3,4},{4,5},{5,6},{6,7},{7,8},{8,9},{9,10},{10,1... | collective-permute-start | bytes 393224 | tf_op jit(solution)/shard_map/ppermute | solution.py:18
  152.6 2.0 copy-start.1
  213.6 7.7 %copy-start.7 = (f32[128,4]{1,0:T(8,128)S(1)}, f32[128,4]{1,0:T(8,128)}, u32[]{:S(2)}) copy-start(f32[128,4]{1,0:T(8,128)} %copy.39) | copy-start | bytes 6148
  221.3 7.2 %copy-start.3 = (bf16[128,2880]{1,0:T(8,128)(2,1)S(1)}, bf16[128,2880]{1,0:T(8,128)(2,1)}, u32[]{:S(2)}) copy-start(bf16[128,2880]{1,0:T(8,128)(2,1)} %copy.33) | copy-start | bytes 2211844
  221.3 8.4 %copy-start.10 = (f32[2880]{0:T(1024)S(1)}, f32[2880]{0:T(1024)}, u32[]{:S(2)}) copy-start(f32[2880]{0:T(1024)} %param.21) | copy-start | bytes 34564
  228.4 23.1 %copy-start.2 = (f32[4,256,128,8]{2,1,3,0:T(8,128)S(1)}, f32[4,256,128,8]{2,1,3,0:T(8,128)}, u32[]{:S(2)}) copy-start(f32[4,256,128,8]{2,1,3,0:T(8,128)} %copy-done.1) | copy-start | bytes 12582916
  228.8 0.9 copy-start.5
  230.3 37.2 %collective-permute-start.1 = (bf16[128,512]{1,0:T(8,128)(2,1)S(1)}, bf16[128,512]{1,0:T(8,128)(2,1)}, u32[]{:S(2)}, u32[]{:S(2)}) collective-permute-start(bf16[128,512]{1,0:T(8,128)(2,1)S(1)} %convolution_convert_fusion.1), channel_id=1, source_target_pairs={{0,7},{1,8},{2,9},{3,10},{4,11},{5,12},{6,13},{7,14},{8,15},{16,23... | collective-permute-start | bytes 393224 | tf_op jit(solution)/shard_map/ppermute | solution.py:18
  250.0 19.7 %collective-permute-start.2 = (bf16[128,512]{1,0:T(8,128)(2,1)S(1)}, bf16[128,512]{1,0:T(8,128)(2,1)S(1)}, u32[]{:S(2)}, u32[]{:S(2)}) collective-permute-start(bf16[128,512]{1,0:T(8,128)(2,1)S(1)} %convolution_convert_fusion.1), channel_id=1, source_target_pairs={{0,6},{1,7},{2,8},{3,9},{4,10},{5,11},{6,12},{7,13},{8,14},{9,15},... | collective-permute-start | bytes 393224 | tf_op jit(solution)/shard_map/ppermute | solution.py:18
  255.4 16.9 %collective-permute-start.3 = (bf16[128,512]{1,0:T(8,128)(2,1)S(1)}, bf16[128,512]{1,0:T(8,128)(2,1)}, u32[]{:S(2)}, u32[]{:S(2)}) collective-permute-start(bf16[128,512]{1,0:T(8,128)(2,1)S(1)} %convolution_convert_fusion.1), channel_id=1, source_target_pairs={{0,5},{1,6},{2,7},{3,8},{4,9},{5,10},{6,11},{7,12},{8,13},{9,14},{... | collective-permute-start | bytes 393224 | tf_op jit(solution)/shard_map/ppermute | solution.py:18
  257.4 15.9 %collective-permute-start.4 = (bf16[128,512]{1,0:T(8,128)(2,1)S(1)}, bf16[128,512]{1,0:T(8,128)(2,1)}, u32[]{:S(2)}, u32[]{:S(2)}) collective-permute-start(bf16[128,512]{1,0:T(8,128)(2,1)S(1)} %convolution_convert_fusion.1), channel_id=1, source_target_pairs={{0,4},{1,5},{2,6},{3,7},{4,8},{5,9},{6,10},{7,11},{8,12},{9,13},{1... | collective-permute-start | bytes 393224 | tf_op jit(solution)/shard_map/ppermute | solution.py:18
  259.3 14.9 %collective-permute-start.5 = (bf16[128,512]{1,0:T(8,128)(2,1)S(1)}, bf16[128,512]{1,0:T(8,128)(2,1)S(1)}, u32[]{:S(2)}, u32[]{:S(2)}) collective-permute-start(bf16[128,512]{1,0:T(8,128)(2,1)S(1)} %convolution_convert_fusion.1), channel_id=1, source_target_pairs={{0,3},{1,4},{2,5},{3,6},{4,7},{5,8},{6,9},{7,10},{8,11},{9,12},{10... | collective-permute-start | bytes 393224 | tf_op jit(solution)/shard_map/ppermute | solution.py:18
  267.5 6.8 %collective-permute-start.6 = (bf16[128,512]{1,0:T(8,128)(2,1)S(1)}, bf16[128,512]{1,0:T(8,128)(2,1)S(1)}, u32[]{:S(2)}, u32[]{:S(2)}) collective-permute-start(bf16[128,512]{1,0:T(8,128)(2,1)S(1)} %convolution_convert_fusion.1), channel_id=1, source_target_pairs={{0,2},{1,3},{2,4},{3,5},{4,6},{5,7},{6,8},{7,9},{8,10},{9,11},{10,... | collective-permute-start | bytes 393224 | tf_op jit(solution)/shard_map/ppermute | solution.py:18
  269.7 4.6 %collective-permute-start.7 = (bf16[128,512]{1,0:T(8,128)(2,1)S(1)}, bf16[128,512]{1,0:T(8,128)(2,1)S(1)}, u32[]{:S(2)}, u32[]{:S(2)}) collective-permute-start(bf16[128,512]{1,0:T(8,128)(2,1)S(1)} %convolution_convert_fusion.1), channel_id=1, source_target_pairs={{0,1},{1,2},{2,3},{3,4},{4,5},{5,6},{6,7},{7,8},{8,9},{9,10},{10,1... | collective-permute-start | bytes 393224 | tf_op jit(solution)/shard_map/ppermute | solution.py:18
  288.8 9.4 %copy-start.6 = (bf16[1024,256]{0,1:T(8,128)(2,1)S(1)}, bf16[1024,256]{0,1:T(8,128)(2,1)}, u32[]{:S(2)}) copy-start(bf16[1024,256]{0,1:T(8,128)(2,1)} %copy.40) | copy-start | bytes 1572868
where the time goes:
time: 315 us; the launch traced here: 309 us
  blocking collectives  75.1 us (24%)
  local copies, waits for them, and re-layouts  60 us (19%)
  matrix products  57.4 us (18%)
  waiting for transfers between devices  43.6 us (14%)
  starting transfers between devices  42.3 us (13%)
  other arithmetic  29.3 us (9%)
    all_to_all x1, blocking collectives, on_device(): lax.all_to_all(copies, 'seq', split_axis=0, concat_axis=0, tiled=True)  75.1 us
    all_to_all x1, waiting for transfers between devices, on_device(): lax.all_to_all(partial_value, 'seq', split_axis=0, concat_axis=0, tiled=T...  43.6 us
    ppermute x8, starting transfers between devices, from_behind(): return lax.ppermute(block, axis, route)  37.5 us
    dot_general x1, matrix products, on_device(): jnp.dot(hidden, down_proj, preferred_element_type=jnp.float32)  26.3 us
    unnamed x38, local copies, waits for them, and re-layouts  21.7 us
    dot_general x2, matrix products, attend(): jnp.einsum('qkgd,skd->kgqs', query_heads, key_heads, preferred_element_ty...  11.1 us
    dot_general x2, matrix products, attend(): jnp.einsum('kgqs,skd->qkgd', weights.astype(jnp.bfloat16), value_heads, p...  10.4 us
    reduce_sum x2, other arithmetic, attend(): totals = jnp.sum(weights, axis=-1)  10.3 us
  transfers between devices with their start and end apart: 9, of which 1 were waited for; matrix products, arithmetic and copies ran while one was open for 6% of the time, Pallas kernels for 0%

commit v1 on v0

v1 whole, which is shorter than its diff:
```python
import functools

import jax
import jax.numpy as jnp
from jax import lax
from jax.experimental import pallas as pl
from jax.experimental.pallas import tpu as pltpu
from jax.sharding import PartitionSpec as P

HEADS = 32
KV_HEADS = 4
HEAD_DIM = 64
EXPERTS = 16
TOP = 4
WINDOW = 128
STRETCH = 1024
LOG2E = 1.4426950408889634
TILE = 512
BUNCH = 4


def tiles(width, tile=TILE):
    return [(at, min(tile, width - at)) for at in range(0, width, tile)]


def normed(values, gain):
    widened = values.astype(jnp.float32)
    second = jnp.mean(widened * widened, axis=-1, keepdims=True)
    return (widened * lax.rsqrt(second + 1e-05) * gain).astype(jnp.bfloat16)


def attend_into(q_ref, read, keys, bias_ref, kx, vx, out_ref):
    half_cols = KV_HEADS * HEAD_DIM
    lane = lax.broadcasted_iota(jnp.int32, (keys, 128), 1) // HEAD_DIM
    pairs = HEADS // KV_HEADS // 2

    @pl.loop(0, KV_HEADS)
    def _(kv):
        side = kv % 2
        for base, ext in ((0, kx), (half_cols, vx)):
            col = pl.multiple_of(base + (kv // 2) * 128, 128)
            both = read(col).astype(jnp.float32)
            same = jnp.where(lane == side, both, 0.0)
            ext[side, 0:keys, :] = same.astype(jnp.bfloat16)
            ext[1 - side, 0:keys, :] = pltpu.roll(same, HEAD_DIM, 1).astype(jnp.bfloat16)

        @pl.loop(0, pairs)
        def _(pair):
            cols = pl.ds(pl.multiple_of((kv * pairs + pair) * 128, 128), 128)
            query = q_ref[:, cols]
            total_out = None
            for parity in range(2):
                scores = lax.dot_general(
                    query, kx[parity, 0:keys, :], (((1,), (1,)), ((), ())),
                    preferred_element_type=jnp.float32,
                ) + bias_ref[...]
                peak = jnp.max(scores, axis=-1, keepdims=True)
                weights = jnp.exp2((scores - peak) * (0.125 * LOG2E))
                totals = jnp.sum(weights, axis=-1, keepdims=True)
                mixed = jnp.dot(
                    weights.astype(jnp.bfloat16), vx[parity, 0:keys, :],
                    preferred_element_type=jnp.float32,
                ) / totals
                total_out = mixed if total_out is None else total_out + mixed
            out_ref[:, cols] = total_out.astype(jnp.bfloat16)


def kernel(
    n, split, back,
    stream, moe_gain, routes_t, gates_t, attn_gain, window_kv,
    window_q_hbm, tract_q_hbm, gate_hbm, up_hbm, down_hbm, proj_hbm,
    window_out, next_out, tract_out,
    wq, tq, wg, wu, wd, wp, send, recv, hid, outs, ret, combine, rim, tkv, ctx, bias_w, bias_t, kx, vx,
    load_sem, send_sem, recv_sem, back_send_sem, back_recv_sem, rim_sem, tract_send, tract_recv,
):
    me = lax.axis_index("seq")
    rows, width = stream.shape
    cap = send.shape[1]
    ff = wg.shape[1]
    loads = [
        pltpu.make_async_copy(src, dst, load_sem.at[i])
        for i, (src, dst) in enumerate(
            ((window_q_hbm, wq), (gate_hbm, wg), (up_hbm, wu), (down_hbm, wd), (proj_hbm, wp), (tract_q_hbm, tq))
        )
    ]

    rim[...] = jnp.zeros_like(rim)
    ctx[...] = jnp.zeros_like(ctx)

    barrier = pltpu.get_barrier_semaphore()

    @pl.loop(1, n)
    def _(d):
        pl.semaphore_signal(barrier, inc=1, device_id={"seq": (me + d) % n}, device_id_type=pl.DeviceIdType.MESH)

    for load in loads:
        load.start()

    expert_id = lax.broadcasted_iota(jnp.int32, (EXPERTS, rows), 0)
    named = jnp.zeros((EXPERTS, rows), jnp.float32)
    gate_of = jnp.zeros((EXPERTS, rows), jnp.float32)
    for k in range(TOP):
        hit = routes_t[k : k + 1, :] == expert_id
        named = named + jnp.where(hit, 1.0, 0.0)
        gate_of = gate_of + jnp.where(hit, gates_t[k : k + 1, :], 0.0)
    earlier = lax.broadcasted_iota(jnp.int32, (rows, rows), 0) < lax.broadcasted_iota(jnp.int32, (rows, rows), 1)
    rank = jnp.dot(
        named.astype(jnp.bfloat16), jnp.where(earlier, 1.0, 0.0).astype(jnp.bfloat16),
        preferred_element_type=jnp.float32,
    )
    rank = jnp.where(named > 0.5, rank, -1.0)
    slot = lax.broadcasted_iota(jnp.int32, (EXPERTS, cap, rows), 1).astype(jnp.float32)
    pick = jnp.where(rank[:, None, :] == slot, 1.0, 0.0)
    moe_input = normed(stream[...], moe_gain[...])
    pick_flat = pick.reshape(EXPERTS * cap, rows).astype(jnp.bfloat16)
    for at, size in tiles(width):
        chosen = jnp.dot(pick_flat, moe_input[:, at : at + size], preferred_element_type=jnp.float32)
        send[:, :, at : at + size] = chosen.astype(jnp.bfloat16).reshape(EXPERTS, cap, size)

    pl.semaphore_wait(barrier, n - 1)

    def dispatch(dst, src):
        return pltpu.make_async_remote_copy(
            src_ref=send.at[dst // split], dst_ref=recv.at[src], send_sem=send_sem.at[dst], recv_sem=recv_sem.at[src],
            device_id={"seq": dst}, device_id_type=pl.DeviceIdType.MESH,
        )

    def give_back(dst, src):
        return pltpu.make_async_remote_copy(
            src_ref=outs.at[dst], dst_ref=ret.at[src], send_sem=back_send_sem.at[dst], recv_sem=back_recv_sem.at[src],
            device_id={"seq": dst}, device_id_type=pl.DeviceIdType.MESH,
        )

    def rim_copy(dst):
        return pltpu.make_async_remote_copy(
            src_ref=window_kv, dst_ref=rim, send_sem=rim_sem.at[0], recv_sem=rim_sem.at[1],
            device_id={"seq": dst}, device_id_type=pl.DeviceIdType.MESH,
        )

    @pl.when(me < n - 1)
    def _():
        rim_copy((me + 1) % n).start()

    @pl.loop(1, n)
    def _(d):
        dispatch((me + d) % n, me).start()

    recv[me] = send[me // split]

    gated = (pick * gate_of[:, None, :])[:, None]
    gated = jnp.broadcast_to(gated, (EXPERTS, split, cap, rows)).reshape(n * cap, rows)
    rest = gated.T
    for i in range(3):
        term = rest.astype(jnp.bfloat16)
        combine[i] = term
        rest = rest - term.astype(jnp.float32)

    row_w = lax.broadcasted_iota(jnp.int32, (rows, rows + WINDOW), 0)
    col_w = lax.broadcasted_iota(jnp.int32, (rows, rows + WINDOW), 1)
    distance = row_w - (col_w - WINDOW)
    seen = (distance >= 0) & (distance < WINDOW) & (me * rows + col_w - WINDOW >= 0)
    bias_w[...] = jnp.where(seen, 0.0, -1e30)
    first = me * rows
    row_t = lax.broadcasted_iota(jnp.int32, bias_t.shape, 0) + first
    col_t = lax.broadcasted_iota(jnp.int32, bias_t.shape, 1) + (first - back * rows)
    lead = STRETCH // 2
    tract = (first + lead) // STRETCH
    start = tract * STRETCH - lead
    seen = (col_t <= row_t) & (col_t >= 0) & (col_t >= start)
    bias_t[...] = jnp.where(seen, 0.0, -1e30)

    loads[0].wait()

    @pl.when(me > 0)
    def _():
        rim_copy((me + n - 1) % n).wait_recv()

    @pl.when(me < n - 1)
    def _():
        rim_copy((me + 1) % n).wait_send()

    def window_cols(col):
        return jnp.concatenate([rim[:, pl.ds(col, 128)], window_kv[:, pl.ds(col, 128)]], 0)

    attend_into(wq, window_cols, rows + WINDOW, bias_w, kx, vx, window_out)

    for load in loads[1:4]:
        load.wait()

    bunches = n // BUNCH

    @pl.loop(0, bunches)
    def _(k):
        base = ((me // BUNCH + k) % bunches) * BUNCH

        @pl.loop(0, BUNCH)
        def _(j):
            @pl.when(base + j != me)
            def _():
                dispatch(base + j, base + j).wait_recv()

        tokens = recv[pl.ds(base, BUNCH)].reshape(BUNCH * cap, width)
        for at, size in tiles(ff):
            gate = jnp.dot(tokens, wg[:, at : at + size], preferred_element_type=jnp.float32)
            up = jnp.dot(tokens, wu[:, at : at + size], preferred_element_type=jnp.float32)
            hid[:, at : at + size] = (gate * jax.nn.sigmoid(gate) * up).astype(jnp.bfloat16)
        for at, size in tiles(width):
            block = jnp.dot(hid[...], wd[:, at : at + size], preferred_element_type=jnp.float32)
            outs[pl.ds(base, BUNCH), :, at : at + size] = block.astype(jnp.bfloat16).reshape(BUNCH, cap, size)

        @pl.loop(0, BUNCH)
        def _(j):
            @pl.when(base + j != me)
            def _():
                give_back(base + j, me).start()

    ret[me] = outs[me]

    @pl.loop(1, n)
    def _(d):
        give_back((me + d) % n, (me + d) % n).wait_recv()

    for at, size in tiles(width):
        total = jnp.zeros((rows, size), jnp.float32)
        returned = ret[:, :, at : at + size].reshape(n * cap, size)
        for i in (2, 1, 0):
            total = total + jnp.dot(combine[i], returned, preferred_element_type=jnp.float32)
        next_out[:, at : at + size] = (stream[:, at : at + size].astype(jnp.float32) + total).astype(jnp.bfloat16)

    for load in loads[4:]:
        load.wait()
    attn_input = normed(next_out[...], attn_gain[...])
    tkv[...] = jnp.dot(attn_input, wp[...], preferred_element_type=jnp.float32).astype(jnp.bfloat16)

    def hand_on(dst, d):
        return pltpu.make_async_remote_copy(
            src_ref=tkv, dst_ref=ctx.at[back - d], send_sem=tract_send.at[d - 1], recv_sem=tract_recv.at[d - 1],
            device_id={"seq": dst}, device_id_type=pl.DeviceIdType.MESH,
        )

    def sends(d):
        return (me + d < n) & (((me + d) * rows + lead) // STRETCH == tract)

    def receives(d):
        return (me - d >= 0) & ((me - d) * rows >= start)

    for d in range(1, back + 1):
        @pl.when(sends(d))
        def _(d=d):
            hand_on((me + d) % n, d).start()

    ctx[back] = tkv[...]
    for d in range(1, back + 1):
        @pl.when(receives(d))
        def _(d=d):
            hand_on((me + n - d) % n, d).wait_recv()

    def tract_cols(col):
        return ctx[:, :, pl.ds(col, 128)].reshape((back + 1) * rows, 128)

    attend_into(tq, tract_cols, (back + 1) * rows, bias_t, kx, vx, tract_out)

    for d in range(1, back + 1):
        @pl.when(sends(d))
        def _(d=d):
            hand_on((me + d) % n, d).wait_send()

    @pl.loop(1, n)
    def _(d):
        dispatch((me + d) % n, me).wait_send()
        give_back((me + d) % n, me).wait_send()


def on_device(
    window_queries, window_kv, stream, moe_gain, routes, route_gates,
    gate_proj, up_proj, down_proj, attn_gain, kv_proj, tract_queries,
):
    n = lax.axis_size("seq")
    rows, width = stream.shape
    split = n // EXPERTS
    cap = rows * TOP // EXPERTS
    ff = gate_proj.shape[1]
    back = STRETCH // rows - 1
    keys = (back + 1) * rows
    vmem = pl.BlockSpec(memory_space=pltpu.VMEM)
    hbm = pl.BlockSpec(memory_space=pl.ANY)
    bf16, f32 = jnp.bfloat16, jnp.float32
    dma = pltpu.SemaphoreType.DMA
    return pl.pallas_call(
        functools.partial(kernel, n, split, back),
        out_shape=(
            jax.ShapeDtypeStruct(window_queries.shape, bf16),
            jax.ShapeDtypeStruct(stream.shape, bf16),
            jax.ShapeDtypeStruct(tract_queries.shape, bf16),
        ),
        in_specs=[vmem] * 6 + [hbm] * 6,
        out_specs=(vmem, vmem, vmem),
        scratch_shapes=[
            pltpu.VMEM(window_queries.shape, bf16),
            pltpu.VMEM(tract_queries.shape, bf16),
            pltpu.VMEM(gate_proj.shape, bf16),
            pltpu.VMEM(up_proj.shape, bf16),
            pltpu.VMEM(down_proj.shape, bf16),
            pltpu.VMEM(kv_proj.shape, bf16),
            pltpu.VMEM((EXPERTS, cap, width), bf16),
            pltpu.VMEM((n, cap, width), bf16),
            pltpu.VMEM((BUNCH * cap, ff), bf16),
            pltpu.VMEM((n, cap, width), bf16),
            pltpu.VMEM((n, cap, width), bf16),
            pltpu.VMEM((3, rows, n * cap), bf16),
            pltpu.VMEM(window_kv.shape, bf16),
            pltpu.VMEM(window_kv.shape, bf16),
            pltpu.VMEM((back + 1,) + window_kv.shape, bf16),
            pltpu.VMEM((rows, rows + WINDOW), f32),
            pltpu.VMEM((rows, keys), f32),
            pltpu.VMEM((2, max(keys, rows + WINDOW), 128), bf16),
            pltpu.VMEM((2, max(keys, rows + WINDOW), 128), bf16),
            dma((6,)), dma((n,)), dma((n,)), dma((n,)), dma((n,)), dma((2,)), dma((max(back, 1),)), dma((max(back, 1),)),
        ],
        compiler_params=pltpu.CompilerParams(
            collective_id=0, has_side_effects=True, vmem_limit_bytes=62 * 2**20
        ),
    )(
        stream, moe_gain[None], routes.T, route_gates.T, attn_gain[None], window_kv,
        window_queries, tract_queries, gate_proj, up_proj, down_proj, kv_proj,
    )


def solution(mesh):
    rows = P(("groups", "seq"), None)
    return jax.shard_map(
        on_device,
        mesh=mesh,
        in_specs=(
            rows, rows, rows, P(), rows, rows,
            P(None, "seq"), P(None, "seq"), P("seq", None), P(), P(), rows,
        ),
        out_specs=(rows, rows, rows),
        check_vma=False,
    )
```

time: 315 us -> 204 us (0.65)
  the two profiles are of different devices: /device:TPU:0 before, /device:TPU:21 now
where the time goes in v1:
time: 204 us; the launch traced here: 203 us
  Pallas kernels  168 us (82%)
  local copies, waits for them, and re-layouts  34.2 us (17%)
    pallas_call x1, Pallas kernels, on_device(): pl.pallas_call(functools.partial(kernel, n, split, back), out_shape=(jax....  168 us
    unnamed x5, local copies, waits for them, and re-layouts  29.3 us

profile of v1, /device:TPU:21, one launch (start us, length us, event | category | flops | bytes accessed | tf_op | source)
XLA Modules:
  0.0 202.7 jit_solution(18412661447082001773)
XLA Ops:
  0.6 1.3 broadcast_in_dim.6.moe_gain
  1.9 1.3 broadcast_in_dim.7.attn_gain
  3.3 2.3 %copy.15.stream = bf16[128,2880]{1,0:T(8,128)(2,1)} copy(bf16[128,2880]{0,1:T(8,128)(2,1)} %param.14) | data formatting | bytes 1474560 | tf_op args[2]
  5.5 11.6 %copy.16.gate_hbm = bf16[2880,1440]{1,0:T(8,128)(2,1)} copy(bf16[2880,1440]{0,1:T(8,128)(2,1)} %param.18) | data formatting | bytes 16588800 | tf_op args[6]
  17.1 11.7 %copy.17.up_hbm = bf16[2880,1440]{1,0:T(8,128)(2,1)} copy(bf16[2880,1440]{0,1:T(8,128)(2,1)} %param.19) | data formatting | bytes 16588800 | tf_op args[7]
  28.8 167.9 %shard_map.139 = (bf16[128,2048]{1,0:T(8,128)(2,1)}, bf16[128,2880]{1,0:T(8,128)(2,1)}, bf16[128,2048]{1,0:T(8,128)(2,1)}) custom-call(bf16[128,2880]{1,0:T(8,128)(2,1)} %copy.15.stream, f32[1,2880]{1,0:T(1,128)} %broadcast_in_dim.6.moe_gain, s32[4,128]{1,0:T(4,128)} %bitcast.2, f32[4,128]{1,0:T(4,128)} %bitcast.3, f32[1,2880]{1,0:T(1,128)} %broadcast_in_dim.7.attn_gain, ...), custom_call_target="tpu_custom_call" | custom-call | tf_op jit(solution)/shard_map/pallas_call | solution.py:289
  196.7 2.3 %copy.18 = bf16[128,2880]{0,1:T(8,128)(2,1)} copy(bf16[128,2880]{1,0:T(8,128)(2,1)} %get-tuple-element.4) | data formatting | bytes 1474560 | tf_op jit(solution)/shard_map/pallas_call | solution.py:289
  199.0 1.9 copy.21
  200.8 1.9 copy.22

commit v2 on v1

--- a/solution.py
+++ b/solution.py
@@ -27,6 +27,10 @@
     widened = values.astype(jnp.float32)
     second = jnp.mean(widened * widened, axis=-1, keepdims=True)
     return (widened * lax.rsqrt(second + 1e-05) * gain).astype(jnp.bfloat16)
+
+
+def dot_rows(left, right):
+    return lax.dot_general(left, right, (((1,), (1,)), ((), ())), preferred_element_type=jnp.float32)
 
 
 def attend_into(q_ref, read, keys, bias_ref, kx, vx, out_ref):
@@ -76,7 +80,7 @@
     me = lax.axis_index("seq")
     rows, width = stream.shape
     cap = send.shape[1]
-    ff = wg.shape[1]
+    ff = wg.shape[0]
     loads = [
         pltpu.make_async_copy(src, dst, load_sem.at[i])
         for i, (src, dst) in enumerate(
@@ -111,7 +115,7 @@
     rank = jnp.where(named > 0.5, rank, -1.0)
     slot = lax.broadcasted_iota(jnp.int32, (EXPERTS, cap, rows), 1).astype(jnp.float32)
     pick = jnp.where(rank[:, None, :] == slot, 1.0, 0.0)
-    moe_input = normed(stream[...], moe_gain[...])
+    moe_input = normed(stream[...], moe_gain[...].reshape(1, width))
     pick_flat = pick.reshape(EXPERTS * cap, rows).astype(jnp.bfloat16)
     for at, size in tiles(width):
         chosen = jnp.dot(pick_flat, moe_input[:, at : at + size], preferred_element_type=jnp.float32)
@@ -201,8 +205,8 @@
 
         tokens = recv[pl.ds(base, BUNCH)].reshape(BUNCH * cap, width)
         for at, size in tiles(ff):
-            gate = jnp.dot(tokens, wg[:, at : at + size], preferred_element_type=jnp.float32)
-            up = jnp.dot(tokens, wu[:, at : at + size], preferred_element_type=jnp.float32)
+            gate = dot_rows(tokens, wg[at : at + size, :])
+            up = dot_rows(tokens, wu[at : at + size, :])
             hid[:, at : at + size] = (gate * jax.nn.sigmoid(gate) * up).astype(jnp.bfloat16)
         for at, size in tiles(width):
             block = jnp.dot(hid[...], wd[:, at : at + size], preferred_element_type=jnp.float32)
@@ -229,7 +233,7 @@
 
     for load in loads[4:]:
         load.wait()
-    attn_input = normed(next_out[...], attn_gain[...])
+    attn_input = normed(next_out[...], attn_gain[...].reshape(1, width))
     tkv[...] = jnp.dot(attn_input, wp[...], preferred_element_type=jnp.float32).astype(jnp.bfloat16)
 
     def hand_on(dst, d):
@@ -298,8 +302,8 @@
         scratch_shapes=[
             pltpu.VMEM(window_queries.shape, bf16),
             pltpu.VMEM(tract_queries.shape, bf16),
-            pltpu.VMEM(gate_proj.shape, bf16),
-            pltpu.VMEM(up_proj.shape, bf16),
+            pltpu.VMEM((ff, width), bf16),
+            pltpu.VMEM((ff, width), bf16),
             pltpu.VMEM(down_proj.shape, bf16),
             pltpu.VMEM(kv_proj.shape, bf16),
             pltpu.VMEM((EXPERTS, cap, width), bf16),
@@ -321,8 +325,8 @@
             collective_id=0, has_side_effects=True, vmem_limit_bytes=62 * 2**20
         ),
     )(
-        stream, moe_gain[None], routes.T, route_gates.T, attn_gain[None], window_kv,
-        window_queries, tract_queries, gate_proj, up_proj, down_proj, kv_proj,
+        stream, moe_gain, routes.T, route_gates.T, attn_gain, window_kv,
+        window_queries, tract_queries, gate_proj.T, up_proj.T, down_proj, kv_proj,
     )
 
 

time: 204 us -> 181 us (0.89)
  local copies, waits for them, and re-layouts: 34.2 us -> 8.27 us
  Pallas kernels: 168 us -> 172 us
    unnamed x5 -> x3, local copies, waits for them, and re-layouts: 29.3 us -> 6.02 us
    pallas_call x1, Pallas kernels: 168 us -> 172 us  [on_device(): pl.pallas_call(functools.partial(kernel, n, split, back), out_shape=(jax....]
    broadcast_in_dim x2 -> x0, local copies, waits for them, and re-layouts: 2.63 us -> none  [the longest x1 1.32 us: on_device(): moe_gain[None]]
where the time goes in v2:
time: 181 us; the launch traced here: 180 us
  Pallas kernels  172 us (95%)
  local copies, waits for them, and re-layouts  8.27 us (5%)
    pallas_call x1, Pallas kernels, on_device(): pl.pallas_call(functools.partial(kernel, n, split, back), out_shape=(jax....  172 us
    unnamed x3, local copies, waits for them, and re-layouts  6.02 us

profile of v2, /device:TPU:21, one launch (start us, length us, event | category | flops | bytes accessed | tf_op | source)
XLA Modules:
  0.0 180.5 jit_solution(11205568460763607741)
XLA Ops:
  0.6 2.3 %copy.15.stream = bf16[128,2880]{1,0:T(8,128)(2,1)} copy(bf16[128,2880]{0,1:T(8,128)(2,1)} %param.14) | data formatting | bytes 1474560 | tf_op args[2]
  2.9 171.6 %shard_map.139 = (bf16[128,2048]{1,0:T(8,128)(2,1)}, bf16[128,2880]{1,0:T(8,128)(2,1)}, bf16[128,2048]{1,0:T(8,128)(2,1)}) custom-call(bf16[128,2880]{1,0:T(8,128)(2,1)} %copy.15.stream, f32[2880]{0:T(1024)} %moe_gain.1, s32[4,128]{1,0:T(4,128)} %bitcast.6, f32[4,128]{1,0:T(4,128)} %bitcast.7, f32[2880]{0:T(1024)} %attn_gain.1, bf16[128,512]{1,0:T(8,128)(2,1)} %window_kv.1, ...), custom_call_target="tpu_custom_call" | custom-call | tf_op jit(solution)/shard_map/pallas_call | solution.py:293
  174.5 2.3 %copy.16 = bf16[128,2880]{0,1:T(8,128)(2,1)} copy(bf16[128,2880]{1,0:T(8,128)(2,1)} %get-tuple-element.4) | data formatting | bytes 1474560 | tf_op jit(solution)/shard_map/pallas_call | solution.py:293
  176.7 1.9 %copy.19 = bf16[128,2048]{1,0:T(8,128)(2,1)} copy(bf16[128,2048]{1,0:T(8,128)(2,1)} %get-tuple-element.9) | data formatting | bytes 1048576
  178.6 1.9 %copy.20 = bf16[128,2048]{1,0:T(8,128)(2,1)} copy(bf16[128,2048]{1,0:T(8,128)(2,1)} %get-tuple-element.11) | data formatting | bytes 1048576

commit v3 on v2

--- a/solution.py
+++ b/solution.py
@@ -71,15 +71,20 @@
 
 def kernel(
     n, split, back,
-    stream, moe_gain, routes_t, gates_t, attn_gain, window_kv,
+    stream, moe_gain, info, attn_gain, window_kv,
     window_q_hbm, tract_q_hbm, gate_hbm, up_hbm, down_hbm, proj_hbm,
     window_out, next_out, tract_out,
-    wq, tq, wg, wu, wd, wp, send, recv, hid, outs, ret, combine, rim, tkv, ctx, bias_w, bias_t, kx, vx,
-    load_sem, send_sem, recv_sem, back_send_sem, back_recv_sem, rim_sem, tract_send, tract_recv,
+    wq, tq, wg, wu, wd, wp, send, recv, hid, outs, ret, combine, mine, theirs, info_p, part, part_in, rim, tkv, ctx, bias_w, bias_t, kx, vx,
+    load_sem, send_sem, recv_sem, back_send_sem, back_recv_sem, rim_sem, pair_sem, tract_send, tract_recv,
 ):
     me = lax.axis_index("seq")
     rows, width = stream.shape
-    cap = send.shape[1]
+    cap = send.shape[2]
+    half = n // 2
+    experts = EXPERTS // 2
+    here = (me // half) * half
+    mate = (me + half) % n
+    place = me - here
     ff = wg.shape[0]
     loads = [
         pltpu.make_async_copy(src, dst, load_sem.at[i])
@@ -100,40 +105,112 @@
     for load in loads:
         load.start()
 
-    expert_id = lax.broadcasted_iota(jnp.int32, (EXPERTS, rows), 0)
-    named = jnp.zeros((EXPERTS, rows), jnp.float32)
-    gate_of = jnp.zeros((EXPERTS, rows), jnp.float32)
-    for k in range(TOP):
-        hit = routes_t[k : k + 1, :] == expert_id
-        named = named + jnp.where(hit, 1.0, 0.0)
-        gate_of = gate_of + jnp.where(hit, gates_t[k : k + 1, :], 0.0)
-    earlier = lax.broadcasted_iota(jnp.int32, (rows, rows), 0) < lax.broadcasted_iota(jnp.int32, (rows, rows), 1)
-    rank = jnp.dot(
-        named.astype(jnp.bfloat16), jnp.where(earlier, 1.0, 0.0).astype(jnp.bfloat16),
-        preferred_element_type=jnp.float32,
-    )
-    rank = jnp.where(named > 0.5, rank, -1.0)
-    slot = lax.broadcasted_iota(jnp.int32, (EXPERTS, cap, rows), 1).astype(jnp.float32)
-    pick = jnp.where(rank[:, None, :] == slot, 1.0, 0.0)
-    moe_input = normed(stream[...], moe_gain[...].reshape(1, width))
-    pick_flat = pick.reshape(EXPERTS * cap, rows).astype(jnp.bfloat16)
-    for at, size in tiles(width):
-        chosen = jnp.dot(pick_flat, moe_input[:, at : at + size], preferred_element_type=jnp.float32)
-        send[:, :, at : at + size] = chosen.astype(jnp.bfloat16).reshape(EXPERTS, cap, size)
+    mine[...] = normed(stream[...], moe_gain[...].reshape(1, width))
 
     pl.semaphore_wait(barrier, n - 1)
 
-    def dispatch(dst, src):
-        return pltpu.make_async_remote_copy(
-            src_ref=send.at[dst // split], dst_ref=recv.at[src], send_sem=send_sem.at[dst], recv_sem=recv_sem.at[src],
-            device_id={"seq": dst}, device_id_type=pl.DeviceIdType.MESH,
-        )
-
-    def give_back(dst, src):
-        return pltpu.make_async_remote_copy(
-            src_ref=outs.at[dst], dst_ref=ret.at[src], send_sem=back_send_sem.at[dst], recv_sem=back_recv_sem.at[src],
-            device_id={"seq": dst}, device_id_type=pl.DeviceIdType.MESH,
-        )
+    def pair_copy(i, src, dst):
+        return pltpu.make_async_remote_copy(
+            src_ref=src, dst_ref=dst, send_sem=pair_sem.at[0, i], recv_sem=pair_sem.at[1, i],
+            device_id={"seq": mate}, device_id_type=pl.DeviceIdType.MESH,
+        )
+
+    info_copy = pair_copy(0, info, info_p)
+    block_copy = pair_copy(1, mine, theirs)
+    part_copy = pair_copy(2, part, part_in)
+    block_copy.start()
+    info_copy.start()
+
+    def dispatch(who, dst, src):
+        return pltpu.make_async_remote_copy(
+            src_ref=send.at[who, (here + dst) // split - here // split], dst_ref=recv.at[who, src],
+            send_sem=send_sem.at[who, dst], recv_sem=recv_sem.at[who, src],
+            device_id={"seq": here + dst}, device_id_type=pl.DeviceIdType.MESH,
+        )
+
+    def give_back(who, dst, src):
+        return pltpu.make_async_remote_copy(
+            src_ref=outs.at[who, dst], dst_ref=ret.at[who, src],
+            send_sem=back_send_sem.at[who, dst], recv_sem=back_recv_sem.at[who, src],
+            device_id={"seq": here + dst}, device_id_type=pl.DeviceIdType.MESH,
+        )
+
+    def spread(who, info_ref, block_ref):
+        first_expert = here // split
+        expert_id = (lax.broadcasted_iota(jnp.int32, (experts, rows), 0) + first_expert).astype(jnp.float32)
+        named = jnp.zeros((experts, rows), jnp.float32)
+        gate_of = jnp.zeros((experts, rows), jnp.float32)
+        for k in range(TOP):
+            hit = info_ref[k : k + 1, :] == expert_id
+            named = named + jnp.where(hit, 1.0, 0.0)
+            gate_of = gate_of + jnp.where(hit, info_ref[TOP + k : TOP + k + 1, :], 0.0)
+        earlier = lax.broadcasted_iota(jnp.int32, (rows, rows), 0) < lax.broadcasted_iota(jnp.int32, (rows, rows), 1)
+        rank = jnp.dot(
+            named.astype(jnp.bfloat16), jnp.where(earlier, 1.0, 0.0).astype(jnp.bfloat16),
+            preferred_element_type=jnp.float32,
+        )
+        rank = jnp.where(named > 0.5, rank, -1.0)
+        slot = lax.broadcasted_iota(jnp.int32, (experts, cap, rows), 1).astype(jnp.float32)
+        pick = jnp.where(rank[:, None, :] == slot, 1.0, 0.0)
+        pick_flat = pick.reshape(experts * cap, rows).astype(jnp.bfloat16)
+        for at, size in tiles(width):
+            chosen = jnp.dot(pick_flat, block_ref[:, at : at + size], preferred_element_type=jnp.float32)
+            send[who, :, :, at : at + size] = chosen.astype(jnp.bfloat16).reshape(experts, cap, size)
+
+        @pl.loop(1, half)
+        def _(d):
+            dispatch(who, (place + d) % half, place).start()
+
+        recv[who, place] = send[who, me // split - here // split]
+        gated = (pick * gate_of[:, None, :])[:, None]
+        gated = jnp.broadcast_to(gated, (experts, split, cap, rows)).reshape(half * cap, rows)
+        rest = gated.T
+        for i in range(3):
+            term = rest.astype(jnp.bfloat16)
+            combine[who, i] = term
+            rest = rest - term.astype(jnp.float32)
+
+    def run(who):
+        bunches = half // BUNCH
+
+        @pl.loop(0, bunches)
+        def _(k):
+            base = ((place // BUNCH + k) % bunches) * BUNCH
+
+            @pl.loop(0, BUNCH)
+            def _(j):
+                @pl.when(base + j != place)
+                def _():
+                    dispatch(who, base + j, base + j).wait_recv()
+
+            tokens = recv[who, pl.ds(base, BUNCH)].reshape(BUNCH * cap, width)
+            for at, size in tiles(ff):
+                gate = dot_rows(tokens, wg[at : at + size, :])
+                up = dot_rows(tokens, wu[at : at + size, :])
+                hid[:, at : at + size] = (gate * jax.nn.sigmoid(gate) * up).astype(jnp.bfloat16)
+            for at, size in tiles(width):
+                block = jnp.dot(hid[...], wd[:, at : at + size], preferred_element_type=jnp.float32)
+                outs[who, pl.ds(base, BUNCH), :, at : at + size] = block.astype(jnp.bfloat16).reshape(BUNCH, cap, size)
+
+            @pl.loop(0, BUNCH)
+            def _(j):
+                @pl.when(base + j != place)
+                def _():
+                    give_back(who, base + j, place).start()
+
+        ret[who, place] = outs[who, place]
+
+    def gathered(who, at, size):
+        total = jnp.zeros((rows, size), jnp.float32)
+        returned = ret[who, :, :, at : at + size].reshape(half * cap, size)
+        for i in (2, 1, 0):
+            total = total + jnp.dot(combine[who, i], returned, preferred_element_type=jnp.float32)
+        return total
+
+    def all_back(who):
+        @pl.loop(1, half)
+        def _(d):
+            give_back(who, (place + d) % half, (place + d) % half).wait_recv()
 
     def rim_copy(dst):
         return pltpu.make_async_remote_copy(
@@ -145,19 +222,7 @@
     def _():
         rim_copy((me + 1) % n).start()
 
-    @pl.loop(1, n)
-    def _(d):
-        dispatch((me + d) % n, me).start()
-
-    recv[me] = send[me // split]
-
-    gated = (pick * gate_of[:, None, :])[:, None]
-    gated = jnp.broadcast_to(gated, (EXPERTS, split, cap, rows)).reshape(n * cap, rows)
-    rest = gated.T
-    for i in range(3):
-        term = rest.astype(jnp.bfloat16)
-        combine[i] = term
-        rest = rest - term.astype(jnp.float32)
+    spread(0, info, mine)
 
     row_w = lax.broadcasted_iota(jnp.int32, (rows, rows + WINDOW), 0)
     col_w = lax.broadcasted_iota(jnp.int32, (rows, rows + WINDOW), 1)
@@ -191,44 +256,19 @@
     for load in loads[1:4]:
         load.wait()
 
-    bunches = n // BUNCH
-
-    @pl.loop(0, bunches)
-    def _(k):
-        base = ((me // BUNCH + k) % bunches) * BUNCH
-
-        @pl.loop(0, BUNCH)
-        def _(j):
-            @pl.when(base + j != me)
-            def _():
-                dispatch(base + j, base + j).wait_recv()
-
-        tokens = recv[pl.ds(base, BUNCH)].reshape(BUNCH * cap, width)
-        for at, size in tiles(ff):
-            gate = dot_rows(tokens, wg[at : at + size, :])
-            up = dot_rows(tokens, wu[at : at + size, :])
-            hid[:, at : at + size] = (gate * jax.nn.sigmoid(gate) * up).astype(jnp.bfloat16)
-        for at, size in tiles(width):
-            block = jnp.dot(hid[...], wd[:, at : at + size], preferred_element_type=jnp.float32)
-            outs[pl.ds(base, BUNCH), :, at : at + size] = block.astype(jnp.bfloat16).reshape(BUNCH, cap, size)
-
-        @pl.loop(0, BUNCH)
-        def _(j):
-            @pl.when(base + j != me)
-            def _():
-                give_back(base + j, me).start()
-
-    ret[me] = outs[me]
-
-    @pl.loop(1, n)
-    def _(d):
-        give_back((me + d) % n, (me + d) % n).wait_recv()
-
+    info_copy.wait()
+    block_copy.wait()
+    spread(1, info_p, theirs)
+    run(0)
+    run(1)
+    all_back(1)
     for at, size in tiles(width):
-        total = jnp.zeros((rows, size), jnp.float32)
-        returned = ret[:, :, at : at + size].reshape(n * cap, size)
-        for i in (2, 1, 0):
-            total = total + jnp.dot(combine[i], returned, preferred_element_type=jnp.float32)
+        part[:, at : at + size] = gathered(1, at, size).astype(jnp.bfloat16)
+    part_copy.start()
+    all_back(0)
+    part_copy.wait_recv()
+    for at, size in tiles(width):
+        total = gathered(0, at, size) + part_in[:, at : at + size].astype(jnp.float32)
         next_out[:, at : at + size] = (stream[:, at : at + size].astype(jnp.float32) + total).astype(jnp.bfloat16)
 
     for load in loads[4:]:
@@ -269,10 +309,12 @@
         def _(d=d):
             hand_on((me + d) % n, d).wait_send()
 
-    @pl.loop(1, n)
-    def _(d):
-        dispatch((me + d) % n, me).wait_send()
-        give_back((me + d) % n, me).wait_send()
+    part_copy.wait_send()
+    for who in range(2):
+        @pl.loop(1, half)
+        def _(d, who=who):
+            dispatch(who, (place + d) % half, place).wait_send()
+            give_back(who, (place + d) % half, place).wait_send()
 
 
 def on_device(
@@ -297,7 +339,7 @@
             jax.ShapeDtypeStruct(stream.shape, bf16),
             jax.ShapeDtypeStruct(tract_queries.shape, bf16),
         ),
-        in_specs=[vmem] * 6 + [hbm] * 6,
+        in_specs=[vmem] * 5 + [hbm] * 6,
         out_specs=(vmem, vmem, vmem),
         scratch_shapes=[
             pltpu.VMEM(window_queries.shape, bf16),
@@ -306,12 +348,17 @@
             pltpu.VMEM((ff, width), bf16),
             pltpu.VMEM(down_proj.shape, bf16),
             pltpu.VMEM(kv_proj.shape, bf16),
-            pltpu.VMEM((EXPERTS, cap, width), bf16),
-            pltpu.VMEM((n, cap, width), bf16),
+            pltpu.VMEM((2, EXPERTS // 2, cap, width), bf16),
+            pltpu.VMEM((2, n // 2, cap, width), bf16),
             pltpu.VMEM((BUNCH * cap, ff), bf16),
-            pltpu.VMEM((n, cap, width), bf16),
-            pltpu.VMEM((n, cap, width), bf16),
-            pltpu.VMEM((3, rows, n * cap), bf16),
+            pltpu.VMEM((2, n // 2, cap, width), bf16),
+            pltpu.VMEM((2, n // 2, cap, width), bf16),
+            pltpu.VMEM((2, 3, rows, n // 2 * cap), bf16),
+            pltpu.VMEM((rows, width), bf16),
+            pltpu.VMEM((rows, width), bf16),
+            pltpu.VMEM((2 * TOP, rows), f32),
+            pltpu.VMEM((rows, width), bf16),
+            pltpu.VMEM((rows, width), bf16),
             pltpu.VMEM(window_kv.shape, bf16),
             pltpu.VMEM(window_kv.shape, bf16),
             pltpu.VMEM((back + 1,) + window_kv.shape, bf16),
@@ -319,13 +366,13 @@
             pltpu.VMEM((rows, keys), f32),
             pltpu.VMEM((2, max(keys, rows + WINDOW), 128), bf16),
             pltpu.VMEM((2, max(keys, rows + WINDOW), 128), bf16),
-            dma((6,)), dma((n,)), dma((n,)), dma((n,)), dma((n,)), dma((2,)), dma((max(back, 1),)), dma((max(back, 1),)),
+            dma((6,)), dma((2, n // 2)), dma((2, n // 2)), dma((2, n // 2)), dma((2, n // 2)), dma((2,)), dma((2, 3)), dma((max(back, 1),)), dma((max(back, 1),)),
         ],
         compiler_params=pltpu.CompilerParams(
             collective_id=0, has_side_effects=True, vmem_limit_bytes=62 * 2**20
         ),
     )(
-        stream, moe_gain, routes.T, route_gates.T, attn_gain, window_kv,
+        stream, moe_gain, jnp.concatenate([routes.T.astype(f32), route_gates.T], 0), attn_gain, window_kv,
         window_queries, tract_queries, gate_proj.T, up_proj.T, down_proj, kv_proj,
     )
 

time: 181 us -> 163 us (0.901)
  Pallas kernels: 172 us -> 151 us
  other arithmetic: 0 us -> 1.96 us
    pallas_call x1, Pallas kernels: 172 us -> 151 us  [on_device(): pl.pallas_call(functools.partial(kernel, n, split, back), out_shape=(jax....]
where the time goes in v3:
time: 163 us; the launch traced here: 162 us
  Pallas kernels  151 us (93%)
  local copies, waits for them, and re-layouts  8.27 us (5%)
  other arithmetic  1.96 us (1%)
    pallas_call x1, Pallas kernels, on_device(): pl.pallas_call(functools.partial(kernel, n, split, back), out_shape=(jax....  151 us
    unnamed x3, local copies, waits for them, and re-layouts  6.01 us

profile of v3, /device:TPU:21, one launch (start us, length us, event | category | flops | bytes accessed | tf_op | source)
XLA Modules:
  0.0 162.3 jit_solution(325216565954385693)
XLA Ops:
  0.6 0.7 convert_bitcast_fusion
  1.3 1.3 pad_maximum_fusion.info
  2.6 2.3 %copy.15.stream = bf16[128,2880]{1,0:T(8,128)(2,1)} copy(bf16[128,2880]{0,1:T(8,128)(2,1)} %param.14) | data formatting | bytes 1474560 | tf_op args[2]
  4.8 151.4 %shard_map.139 = (bf16[128,2048]{1,0:T(8,128)(2,1)}, bf16[128,2880]{1,0:T(8,128)(2,1)}, bf16[128,2048]{1,0:T(8,128)(2,1)}) custom-call(bf16[128,2880]{1,0:T(8,128)(2,1)} %copy.15.stream, f32[2880]{0:T(1024)} %moe_gain.1, f32[8,128]{1,0:T(8,128)} %pad_maximum_fusion.info, f32[2880]{0:T(1024)} %attn_gain.1, bf16[128,512]{1,0:T(8,128)(2,1)} %window_kv.1, ...), custom_call_target="tpu_custom_call" | custom-call | tf_op jit(solution)/shard_map/pallas_call | solution.py:335
  156.2 2.3 %copy.16 = bf16[128,2880]{0,1:T(8,128)(2,1)} copy(bf16[128,2880]{1,0:T(8,128)(2,1)} %get-tuple-element.4) | data formatting | bytes 1474560 | tf_op jit(solution)/shard_map/pallas_call | solution.py:335
  158.5 1.9 %copy.19 = bf16[128,2048]{1,0:T(8,128)(2,1)} copy(bf16[128,2048]{1,0:T(8,128)(2,1)} %get-tuple-element.9) | data formatting | bytes 1048576
  160.4 1.9 %copy.20 = bf16[128,2048]{1,0:T(8,128)(2,1)} copy(bf16[128,2048]{1,0:T(8,128)(2,1)} %get-tuple-element.11) | data formatting | bytes 1048576
